TPU v7x, 32 devices: a whole 2x2x4 slice. The times are simulated.
32 devices in a mesh: row: 8 (over y, x, core), col: 4 (over z).
Axes of the slice: x: 2, y: 2, z: 4, core: 2. Of those that a mesh axis runs over, the one named last changes fastest.
Arguments:
- node_features: bfloat16 [8192, 512], P(('col', 'row')), may hold values from -6 to 6
- tile_values: bfloat16 [8, 192, 128, 128], P('row', 'col'), may hold values from -0.15625 to 0.15625
- tile_rows: int32 [8, 192], P('row', 'col'), may hold values from 0 to 7, as said below
- tile_cols: int32 [8, 192], P('row', 'col'), may hold values from 0 to 15, as said below
- tile_count: int32 [8, 4], P('row', 'col'), may hold values from 1 to 48, as said below
- weight: bfloat16 [512, 512], replicated, may hold values from -0.25 to 0.25
- bias: float32 [512], replicated, may hold values from -3 to 3
- cotangent: bfloat16 [8192, 512], P(('row', 'col')), may hold values from -6 to 6
Outputs:
- output: bfloat16 [8192, 512], P(('row', 'col'))
- feature_grad: bfloat16 [8192, 512], P(('col', 'row'))
- weight_grad: float32 [512, 512], replicated
- bias_grad: float32 [512], replicated
Inputs may be any that keep to these rules, and one draw needn't show every extreme that they name: `tile_rows`: within one grid block the used slots name distinct tiles; together with tile_cols each slot names one tile of the block. `tile_cols`: within one grid block the used slots name distinct tiles. `tile_count`: some grid block uses all 48 slots.
All inputs are finite; a program needn't handle non-finite values.
Results may differ from a plain program's by a relative error of at most 0.014.
Values may be sent and summed in bfloat16 or wider, within the bound.
A program may use at most 128 MiB of HBM per device.

v0:
```python
import math

import jax
import jax.numpy as jnp
from jax import lax
from jax.sharding import PartitionSpec as P


def grouped_product(blocks, out_index, in_index, tile_total, operand, out_tiles, transposed):
    tile_size = blocks.shape[-1]
    features = operand.shape[-1]
    group_size = math.gcd(blocks.shape[0], 32)
    panels = operand.reshape(operand.shape[0] // tile_size, tile_size, features)
    einsum_form = "tji,tjf->tif" if transposed else "tij,tjf->tif"

    def step(step_index, running):
        first_slot = step_index * group_size
        tile_piece = lax.dynamic_slice_in_dim(blocks, first_slot, group_size, 0)
        target = lax.dynamic_slice_in_dim(out_index, first_slot, group_size, 0)
        source = lax.dynamic_slice_in_dim(in_index, first_slot, group_size, 0)
        in_range = first_slot + jnp.arange(group_size) < tile_total
        product = jnp.einsum(
            einsum_form, tile_piece, panels[source], preferred_element_type=jnp.float32
        )
        product = jnp.where(in_range[:, None, None], product, jnp.float32(0.0))
        return running.at[target].add(product)

    steps_needed = (tile_total + group_size - 1) // group_size
    initial = jnp.zeros((out_tiles, tile_size, features), jnp.float32)
    result = lax.fori_loop(0, steps_needed, step, initial)
    return result.reshape(out_tiles * tile_size, features)


def per_device(
    node_features, tile_values, tile_rows, tile_cols, tile_count, weight, bias, cotangent
):
    blocks = tile_values[0]
    row_index = tile_rows[0]
    col_index = tile_cols[0]
    tile_total = tile_count[0, 0]
    tile_size = blocks.shape[-1]
    local_nodes = node_features.shape[0]
    row_tiles = local_nodes * lax.axis_size("col") // tile_size
    col_tiles = local_nodes * lax.axis_size("row") // tile_size
    node_total = local_nodes * lax.axis_size("row") * lax.axis_size("col")
    contract = (((0,), (0,)), ((), ()))
    back_form = (((1,), (1,)), ((), ()))
    node_panel = lax.all_gather(node_features, "row", axis=0, tiled=True)
    partial_value = grouped_product(
        blocks, row_index, col_index, tile_total, node_panel, row_tiles, False
    )
    aggregated = lax.psum_scatter(partial_value, "col", scatter_dimension=0, tiled=True).astype(
        jnp.bfloat16
    )
    pre_act = jnp.dot(aggregated, weight, preferred_element_type=jnp.float32) + bias
    sigmoid_pre = jax.nn.sigmoid(pre_act)
    output = (pre_act * sigmoid_pre).astype(jnp.bfloat16)
    grad_pre = (
        cotangent.astype(jnp.float32) * sigmoid_pre * (1.0 + pre_act * (1.0 - sigmoid_pre))
    ).astype(jnp.bfloat16)
    weight_local = lax.dot_general(
        aggregated, grad_pre, contract, preferred_element_type=jnp.float32
    )
    bias_local = jnp.sum(grad_pre.astype(jnp.float32), axis=0)
    weight_sum, bias_sum = lax.psum((weight_local, bias_local), ("row", "col"))
    grad_scale = 1.0 / math.sqrt(node_total)
    local_grads = lax.dot_general(
        grad_pre, weight, back_form, preferred_element_type=jnp.float32
    ).astype(jnp.bfloat16)
    row_grads = lax.all_gather(local_grads, "col", axis=0, tiled=True)
    column_partial = grouped_product(
        blocks, col_index, row_index, tile_total, row_grads, col_tiles, True
    )
    feature_grad = lax.psum_scatter(
        column_partial.astype(jnp.bfloat16), "row", scatter_dimension=0, tiled=True
    )
    return (output, feature_grad, weight_sum * grad_scale, bias_sum * grad_scale)


def solution(mesh):
    return jax.shard_map(
        per_device,
        mesh=mesh,
        in_specs=(
            P(("col", "row"), None),
            P("row", "col", None, None),
            P("row", "col"),
            P("row", "col"),
            P("row", "col"),
            P(),
            P(),
            P(("row", "col"), None),
        ),
        out_specs=(P(("row", "col"), None), P(("col", "row"), None), P(), P()),
        check_vma=False,
    )
```

profile of v0, /device:TPU:0, one launch (start us, length us, event | category | flops | bytes accessed | tf_op | source)
XLA Modules:
  0.0 348.0 jit_solution(5711596668636488482)
XLA Ops:
  7.2 0.0 copy-start
  7.2 0.0 copy-start.4
  7.2 0.0 copy-start.5
  7.2 0.0 all-gather.3.cloned.1.call-start
  7.2 0.7 all-gather.3.cloned.1.call-update
  7.9 0.0 reduce-scatter.3.cloned.1.call-start
  8.7 31.9 %all-gather.3.cloned.1.call-done = bf16[2048,512]{1,0:T(8,128)(2,1)} async-done(((bf16[256,512]{1,0:T(8,128)(2,1)}), bf16[2048,512]{1,0:T(8,128)(2,1)}) %all-gather.3.cloned.1.call-update) | async-done | bytes 2097168 | tf_op jit(solution)/shard_map/all_gather | solution.py:48
  40.6 0.2 broadcast_in_dim.41
  40.8 44.9 %while.20 = (s32[]{:T(128)}, f32[8,128,512]{2,1,0:T(8,128)S(1)}, s32[]{:T(128)}, s32[48]{0:T(128)S(1)}, s32[]{:T(128)}, /*index=5*/bf16[48,128,128]{2,1,0:T(8,12...) while((s32[]{:T(128)}, f32[8,128,512]{2,1,0:T(8,128)S(1)}, ...), condition=%wide.region_2.3_spmd, body=%wide.region_0.2_spmd.sunk | while | flops 270533760 | bytes 23597716 | solution.py:30
  40.9 0.1 compare_select_fusion.6
  40.9 3.6 %gather_fusion = bf16[16,128,512]{2,1,0:T(8,128)(2,1)} fusion(bf16[16,128,512]{2,1,0:T(8,128)(2,1)} %get-tuple-element.278, s32[1024]{0:T(1024)S(1)} %pad_clamp_fusion.4), kind=kCustom, calls=%fused_computation.clone.1 | custom fusion | bytes 4194368 | tf_op jit(solution)/shard_map/while/body/gather | solution.py:23
  44.6 0.7 add_compare_fusion.4
  45.2 4.4 %convolution_select_fusion.4 = f32[16,128,512]{2,1,0:T(8,128)} fusion(bf16[16,128,512]{2,1,0:T(8,128)(2,1)} %gather_fusion, pred[16]{0:T(512)(128)(4,1)S(1)} %add_compare_fusion.4, bf16[48,128,128]{2,1,0:T(8,128)(2,1)} %get-tuple-element.276, s32[]{:T(128)S(6)} %select_n.50), kind=kOutput, calls=%fused_computation.4.clone.1 | convolution fusion | flops 269484032 | bytes 6815764 | tf_op jit(solution)/shard_map/while/body/tij,tjf->tif/dot_general | solution.py:22
  49.6 6.1 %scatter_fusion = f32[8,128,512]{2,1,0:T(8,128)S(1)} fusion(f32[8,128,512]{2,1,0:T(8,128)S(1)} %get-tuple-element.260, s32[16]{0:T(128)S(1)} %get-tuple-element.235, f32[16,128,512]{2,1,0:T(8,128)} %convolution_select_fusion.4), kind=kCustom, calls=%fused_computation.2.clone.1 | custom fusion | flops 1048576 | bytes 12582976 | tf_op jit(solution)/shard_map/while/body/scatter-add | solution.py:26
  55.8 0.1 compare_select_fusion.6
  55.9 3.6 %gather_fusion = bf16[16,128,512]{2,1,0:T(8,128)(2,1)} fusion(bf16[16,128,512]{2,1,0:T(8,128)(2,1)} %get-tuple-element.278, s32[1024]{0:T(1024)S(1)} %pad_clamp_fusion.4), kind=kCustom, calls=%fused_computation.clone.1 | custom fusion | bytes 4194368 | tf_op jit(solution)/shard_map/while/body/gather | solution.py:23
  59.5 0.7 add_compare_fusion.4
  60.2 4.4 %convolution_select_fusion.4 = f32[16,128,512]{2,1,0:T(8,128)} fusion(bf16[16,128,512]{2,1,0:T(8,128)(2,1)} %gather_fusion, pred[16]{0:T(512)(128)(4,1)S(1)} %add_compare_fusion.4, bf16[48,128,128]{2,1,0:T(8,128)(2,1)} %get-tuple-element.276, s32[]{:T(128)S(6)} %select_n.50), kind=kOutput, calls=%fused_computation.4.clone.1 | convolution fusion | flops 269484032 | bytes 6815764 | tf_op jit(solution)/shard_map/while/body/tij,tjf->tif/dot_general | solution.py:22
  64.6 6.2 %scatter_fusion = f32[8,128,512]{2,1,0:T(8,128)S(1)} fusion(f32[8,128,512]{2,1,0:T(8,128)S(1)} %get-tuple-element.260, s32[16]{0:T(128)S(1)} %get-tuple-element.235, f32[16,128,512]{2,1,0:T(8,128)} %convolution_select_fusion.4), kind=kCustom, calls=%fused_computation.2.clone.1 | custom fusion | flops 1048576 | bytes 12582976 | tf_op jit(solution)/shard_map/while/body/scatter-add | solution.py:26
  70.8 0.1 compare_select_fusion.6
  70.9 3.6 %gather_fusion = bf16[16,128,512]{2,1,0:T(8,128)(2,1)} fusion(bf16[16,128,512]{2,1,0:T(8,128)(2,1)} %get-tuple-element.278, s32[1024]{0:T(1024)S(1)} %pad_clamp_fusion.4), kind=kCustom, calls=%fused_computation.clone.1 | custom fusion | bytes 4194368 | tf_op jit(solution)/shard_map/while/body/gather | solution.py:23
  74.5 0.7 add_compare_fusion.4
  75.2 4.4 %convolution_select_fusion.4 = f32[16,128,512]{2,1,0:T(8,128)} fusion(bf16[16,128,512]{2,1,0:T(8,128)(2,1)} %gather_fusion, pred[16]{0:T(512)(128)(4,1)S(1)} %add_compare_fusion.4, bf16[48,128,128]{2,1,0:T(8,128)(2,1)} %get-tuple-element.276, s32[]{:T(128)S(6)} %select_n.50), kind=kOutput, calls=%fused_computation.4.clone.1 | convolution fusion | flops 269484032 | bytes 6815764 | tf_op jit(solution)/shard_map/while/body/tij,tjf->tif/dot_general | solution.py:22
  79.6 6.2 %scatter_fusion = f32[8,128,512]{2,1,0:T(8,128)S(1)} fusion(f32[8,128,512]{2,1,0:T(8,128)S(1)} %get-tuple-element.260, s32[16]{0:T(128)S(1)} %get-tuple-element.235, f32[16,128,512]{2,1,0:T(8,128)} %convolution_select_fusion.4), kind=kCustom, calls=%fused_computation.2.clone.1 | custom fusion | flops 1048576 | bytes 12582976 | tf_op jit(solution)/shard_map/while/body/scatter-add | solution.py:26
  85.8 0.0 copy-start.6
  85.8 0.0 copy-start.7
  85.8 1.3 copy-done.1
  87.1 0.0 reduce-scatter.3.cloned.1.call-update
  87.1 0.0 copy-start.2
  87.1 0.0 all-gather.5.cloned.1.call-start
  87.2 43.8 %reduce-scatter.3.cloned.1.call-done = f32[256,512]{1,0:T(8,128)} async-done(((f32[1024,512]{1,0:T(8,128)}), f32[256,512]{1,0:T(8,128)}) %reduce-scatter.3.cloned.1.call-update) | async-done | bytes 524304 | tf_op jit(solution)/shard_map/reduce_scatter | solution.py:52
  131.0 2.3 convert_reduce_fusion
  133.3 1.0 convolution_convert_fusion
  134.3 0.0 all-gather.5.cloned.1.call-update
  134.4 0.0 all-reduce.2.cloned.1.call-start
  134.4 1.6 copy.12
  136.0 1.3 fusion.4
  137.3 0.0 all-reduce.2.cloned.1.call-update
  137.4 0.0 reduce-scatter.5.cloned.1.call-start
  137.4 24.4 %all-gather.5.cloned.1.call-done = bf16[1024,512]{1,0:T(8,128)(2,1)} async-done(((bf16[256,512]{1,0:T(8,128)(2,1)}), bf16[1024,512]{1,0:T(8,128)(2,1)}) %all-gather.5.cloned.1.call-update) | async-done | bytes 1048592 | tf_op jit(solution)/shard_map/all_gather | solution.py:70
  161.8 2.5 broadcast_in_dim.42
  164.3 47.4 %while.21 = (s32[]{:T(128)}, f32[16,128,512]{2,1,0:T(8,128)}, s32[]{:T(128)}, s32[48]{0:T(128)S(1)}, s32[]{:T(128)}, /*index=5*/bf16[48,128,128]{1,2,0:T(8,128)(...) while((s32[]{:T(128)}, f32[16,128,512]{2,1,0:T(8,128)}, ...), condition=%wide.region_6.7_spmd, body=%wide.region_4.6_spmd.sunk | while | flops 270533760 | bytes 23597716 | solution.py:30
  164.3 0.1 compare_select_fusion.7
  164.4 1.9 gather_fusion.1
  166.3 0.7 add_compare_fusion.5
  166.9 3.7 %convolution_select_fusion.5 = f32[16,128,512]{2,1,0:T(8,128)} fusion(bf16[16,128,512]{2,1,0:T(8,128)(2,1)S(1)} %gather_fusion.1, pred[16]{0:T(512)(128)(4,1)S(1)} %add_compare_fusion.5, bf16[48,128,128]{1,2,0:T(8,128)(2,1)} %get-tuple-element.312, s32[]{:T(128)S(6)} %select_n.53), kind=kOutput, calls=%fused_computation.11.clone.1 | convolution fusion | flops 269484032 | bytes 6815764 | tf_op jit(solution)/shard_map/while/body/tji,tjf->tif/dot_general | solution.py:22
  170.6 9.5 %scatter_fusion.1 = f32[16,128,512]{2,1,0:T(8,128)} fusion(f32[16,128,512]{2,1,0:T(8,128)} %get-tuple-element.296, s32[16]{0:T(128)S(1)} %get-tuple-element.245, f32[16,128,512]{2,1,0:T(8,128)} %convolution_select_fusion.5), kind=kCustom, calls=%fused_computation.3.clone.1 | custom fusion | flops 1048576 | bytes 12582976 | tf_op jit(solution)/shard_map/while/body/scatter-add | solution.py:26
  180.1 0.1 compare_select_fusion.7
  180.2 1.9 gather_fusion.1
  182.1 0.7 add_compare_fusion.5
  182.8 3.7 %convolution_select_fusion.5 = f32[16,128,512]{2,1,0:T(8,128)} fusion(bf16[16,128,512]{2,1,0:T(8,128)(2,1)S(1)} %gather_fusion.1, pred[16]{0:T(512)(128)(4,1)S(1)} %add_compare_fusion.5, bf16[48,128,128]{1,2,0:T(8,128)(2,1)} %get-tuple-element.312, s32[]{:T(128)S(6)} %select_n.53), kind=kOutput, calls=%fused_computation.11.clone.1 | convolution fusion | flops 269484032 | bytes 6815764 | tf_op jit(solution)/shard_map/while/body/tji,tjf->tif/dot_general | solution.py:22
  186.5 9.4 %scatter_fusion.1 = f32[16,128,512]{2,1,0:T(8,128)} fusion(f32[16,128,512]{2,1,0:T(8,128)} %get-tuple-element.296, s32[16]{0:T(128)S(1)} %get-tuple-element.245, f32[16,128,512]{2,1,0:T(8,128)} %convolution_select_fusion.5), kind=kCustom, calls=%fused_computation.3.clone.1 | custom fusion | flops 1048576 | bytes 12582976 | tf_op jit(solution)/shard_map/while/body/scatter-add | solution.py:26
  195.9 0.1 compare_select_fusion.7
  195.9 1.9 gather_fusion.1
  197.9 0.7 add_compare_fusion.5
  198.5 3.7 %convolution_select_fusion.5 = f32[16,128,512]{2,1,0:T(8,128)} fusion(bf16[16,128,512]{2,1,0:T(8,128)(2,1)S(1)} %gather_fusion.1, pred[16]{0:T(512)(128)(4,1)S(1)} %add_compare_fusion.5, bf16[48,128,128]{1,2,0:T(8,128)(2,1)} %get-tuple-element.312, s32[]{:T(128)S(6)} %select_n.53), kind=kOutput, calls=%fused_computation.11.clone.1 | convolution fusion | flops 269484032 | bytes 6815764 | tf_op jit(solution)/shard_map/while/body/tji,tjf->tif/dot_general | solution.py:22
  202.2 9.5 %scatter_fusion.1 = f32[16,128,512]{2,1,0:T(8,128)} fusion(f32[16,128,512]{2,1,0:T(8,128)} %get-tuple-element.296, s32[16]{0:T(128)S(1)} %get-tuple-element.245, f32[16,128,512]{2,1,0:T(8,128)} %convolution_select_fusion.5), kind=kCustom, calls=%fused_computation.3.clone.1 | custom fusion | flops 1048576 | bytes 12582976 | tf_op jit(solution)/shard_map/while/body/scatter-add | solution.py:26
  211.7 3.8 %convert_element_type.29 = bf16[16,128,512]{2,1,0:T(8,128)(2,1)} convert(f32[16,128,512]{2,1,0:T(8,128)} %get-tuple-element.91) | non-fusion elementwise | flops 1048576 | bytes 6291456 | tf_op jit(solution)/shard_map/convert_element_type | solution.py:75
  215.5 0.0 reduce-scatter.5.cloned.1.call-update
  215.6 39.5 %psum.15 = f32[512]{0:T(512)S(1)} all-reduce(f32[512]{0:T(512)S(1)} %get-tuple-element.132), channel_id=1, replica_groups=mesh['row'=8,'col'=4] {'row','col'}, use_global_device_ids=true, to_apply=%region_10.11 | all-reduce | flops 512 | bytes 4096 | tf_op jit(solution)/shard_map/psum | solution.py:65
  255.1 0.6 broadcast_multiply_fusion.1
  255.6 41.9 %all-reduce.2.cloned.1.call-done = f32[512,512]{1,0:T(8,128)} async-done(((f32[512,512]{1,0:T(8,128)}), f32[512,512]{1,0:T(8,128)}) %all-reduce.2.cloned.1.call-update) | async-done | bytes 1048592 | tf_op jit(solution)/shard_map/psum | solution.py:65
  297.6 2.3 broadcast_multiply_fusion
  299.9 41.6 %reduce-scatter.5.cloned.1.call-done = bf16[256,512]{1,0:T(8,128)(2,1)} async-done(((bf16[2048,512]{1,0:T(8,128)(2,1)}), bf16[256,512]{1,0:T(8,128)(2,1)}) %reduce-scatter.5.cloned.1.call-update) | async-done | bytes 262160 | tf_op jit(solution)/shard_map/reduce_scatter | solution.py:74
  (15 shorter events, 0.1 us)
Async XLA Ops:
  7.2 123.9 %copy-start = (bf16[512,512]{1,0:T(8,128)(2,1)S(1)}, bf16[512,512]{1,0:T(8,128)(2,1)}, u32[]{:S(2)}) copy-start(bf16[512,512]{1,0:T(8,128)(2,1)} %param.17) | copy-start | bytes 1572868
  7.2 33.6 %copy-start.4 = (s32[1,48]{1,0:T(1,128)S(1)}, s32[1,48]{1,0:T(1,128)}, u32[]{:S(2)}) copy-start(s32[1,48]{1,0:T(1,128)} %param.14) | copy-start | bytes 580
  7.2 33.6 %copy-start.5 = (s32[1,48]{1,0:T(1,128)S(1)}, s32[1,48]{1,0:T(1,128)}, u32[]{:S(2)}) copy-start(s32[1,48]{1,0:T(1,128)} %param.15) | copy-start | bytes 580
  7.2 33.4 %all-gather.3.cloned.1.call-start = ((), (), s32[]{:S(2)}) async-start(), calls=%async_computation.2 | async-start | bytes 2359296 | tf_op jit(solution)/shard_map/all_gather | solution.py:48
  7.9 123.1 %reduce-scatter.3.cloned.1.call-start = ((), (), s32[]{:S(2)}) async-start(), calls=%async_computation.3 | async-start | bytes 2621440 | tf_op jit(solution)/shard_map/reduce_scatter | solution.py:52
  85.8 1.3 copy-start.1
  85.8 45.3 %copy-start.6 = (bf16[256,512]{1,0:T(8,128)(2,1)S(1)}, bf16[256,512]{1,0:T(8,128)(2,1)}, u32[]{:S(2)}) copy-start(bf16[256,512]{1,0:T(8,128)(2,1)} %param.19) | copy-start | bytes 786436
  85.8 45.3 %copy-start.7 = (f32[512]{0:T(512)S(1)}, f32[512]{0:T(512)}, u32[]{:S(2)}) copy-start(f32[512]{0:T(512)} %param.18) | copy-start | bytes 6148
  87.1 47.3 %copy-start.2 = (bf16[48,128,128]{2,1,0:T(8,128)(2,1)S(1)}, bf16[48,128,128]{2,1,0:T(8,128)(2,1)}, u32[]{:S(2)}) copy-start(bf16[48,128,128]{2,1,0:T(8,128)(2,1)} %get-tuple-element.328) | copy-start | bytes 4718596
  87.1 74.6 %all-gather.5.cloned.1.call-start = ((), (), s32[]{:S(2)}) async-start(), calls=%async_computation.4 | async-start | bytes 1310720 | tf_op jit(solution)/shard_map/all_gather | solution.py:70
  133.3 2.7 copy-start.3
  134.4 163.2 %all-reduce.2.cloned.1.call-start = ((), (), s32[]{:S(2)}) async-start(), calls=%async_computation.6 | async-start | bytes 2097152 | tf_op jit(solution)/shard_map/psum | solution.py:65
  137.4 204.1 %reduce-scatter.5.cloned.1.call-start = ((), (), s32[]{:S(2)}) async-start(), calls=%async_computation.5 | async-start | bytes 2359296 | tf_op jit(solution)/shard_map/reduce_scatter | solution.py:74
Sparse Core Ops, SparseCore 0:
  9.9 30.5 all-gather.2
  87.2 43.7 reduce-scatter.2
  134.5 27.2 all-gather.4
  168.2 129.3 all-reduce.1
  301.3 40.1 reduce-scatter.4
where the time goes:
time: 349 us; the launch traced here: 348 us
  waiting for transfers between devices  184 us (53%)
  other arithmetic  58 us (17%)
  blocking collectives  39.5 us (11%)
  matrix products  28.9 us (8%)
  local copies, waits for them, and re-layouts  22.4 us (6%)
  between operations  14.5 us (4%)
    scatter-add x6, other arithmetic, step(): return running.at[target].add(product)  46.8 us
    reduce_scatter x1, waiting for transfers between devices, per_device(): lax.psum_scatter(partial_value, 'col', scatter_dimension=0, tiled=True)  43.8 us
    psum x1, waiting for transfers between devices, per_device(): weight_sum, bias_sum = lax.psum((weight_local, bias_local), ('row', 'col'))  41.9 us
    reduce_scatter x1, waiting for transfers between devices, per_device(): lax.psum_scatter(column_partial.astype(jnp.bfloat16), 'row', scatter_dime...  41.6 us
    psum x1, blocking collectives, per_device(): weight_sum, bias_sum = lax.psum((weight_local, bias_local), ('row', 'col'))  39.5 us
    all_gather x1, waiting for transfers between devices, per_device(): node_panel = lax.all_gather(node_features, 'row', axis=0, tiled=True)  31.9 us
    all_gather x1, waiting for transfers between devices, per_device(): row_grads = lax.all_gather(local_grads, 'col', axis=0, tiled=True)  24.4 us
    dot_general x6, matrix products, step(): jnp.einsum(einsum_form, tile_piece, panels[source], preferred_element_typ...  24.3 us
  transfers between devices with their start and end apart: 5, of which 5 were waited for; matrix products, arithmetic and copies ran while one was open for 17% of the time, Pallas kernels for 0%

commit v1 on v0

v1 whole, which is shorter than its diff:
```python
import functools
import math

import jax
import jax.numpy as jnp
from jax import lax
from jax.experimental import pallas as pl
from jax.experimental.pallas import tpu as pltpu
from jax.sharding import PartitionSpec as P

MESH = pl.DeviceIdType.MESH
BIAS_ROWS = 16


def layer_kernel(
    n_row, n_col, n_chunk,
    slot_ref, x_ref, tiles_hbm, w_hbm, bias_ref, ct_hbm,
    out_ref, fg_ref, wg_ref, bg_ref,
    tiles, a_blk, at_blk, w_ref, ct_ref, xg, part, part_in, own, agg, gp_ref, gg,
    sib_in, tot_in, wb_out, wb_in, wz, wfin,
    local_sem, xl_sem, xs_sem, xf_sem, xr_sem, ps_sem, pr_sem, gs_sem, gr_sem,
    ss_sem, sr_sem, ts_sem, tr_sem, ws_sem, wr_sem, zs_sem, zr_sem, fs_sem, fr_sem,
):
    f32, bf16 = jnp.float32, jnp.bfloat16
    tile_slots = tiles_hbm.shape[0]
    tile = tiles_hbm.shape[1]
    length, features = x_ref.shape
    width = features // n_chunk
    row_tiles = length * n_col // tile
    col_tiles = length * n_row // tile
    n_chip = n_row // 2
    w_rows = features // n_row

    me_r, me_c = lax.axis_index("row"), lax.axis_index("col")
    chip, core = me_r // 2, me_r % 2
    sib = me_r + 1 - 2 * core

    def rows(i):
        return pl.ds(pl.multiple_of(i * length, length), length)

    def remote(src, dst, send, recv, **where):
        return pltpu.make_async_remote_copy(
            src_ref=src, dst_ref=dst, send_sem=send, recv_sem=recv,
            device_id=where, device_id_type=MESH,
        )

    def other_chip(k):
        return lax.rem(chip + k, n_chip)

    def other_col(k):
        return lax.rem(me_c + k, n_col)

    def other_row(k):
        return lax.rem(me_r + k, n_row)

    tiles_copy = pltpu.make_async_copy(tiles_hbm, tiles.at[pl.ds(0, tile_slots)], local_sem.at[0])
    w_copy = pltpu.make_async_copy(w_hbm, w_ref, local_sem.at[1])
    ct_copy = pltpu.make_async_copy(ct_hbm, ct_ref, local_sem.at[2])
    tiles_copy.start()

    def x_chunk(c):
        return x_ref.at[:, pl.ds(c * width, width)]

    def x_local(c):
        return pltpu.make_async_copy(x_chunk(c), xg.at[c, rows(me_r)], xl_sem.at[c])

    for c in range(n_chunk):
        x_local(c).start()
    w_copy.start()
    ct_copy.start()

    barrier = pltpu.get_barrier_semaphore()
    for k in range(1, n_row):
        pl.semaphore_signal(barrier, inc=1, device_id={"row": other_row(k)}, device_id_type=MESH)
    for k in range(1, n_col):
        pl.semaphore_signal(barrier, inc=1, device_id={"col": other_col(k)}, device_id_type=MESH)
    pl.semaphore_wait(barrier, n_row + n_col - 2)

    def x_send(c, k):
        return remote(x_chunk(c), xg.at[c, rows(me_r)], xs_sem.at[c, k], xr_sem.at[c, me_r],
                      row=2 * other_chip(k) + core)

    def x_sib(c):
        return remote(x_chunk(c), xg.at[c, rows(me_r)], xs_sem.at[c, 0], xr_sem.at[c, me_r], row=sib)

    def x_forward(c, k):
        src = 2 * other_chip(n_chip - k) + core
        block = xg.at[c, rows(src)]
        return remote(block, block, xf_sem.at[c, k - 1], xr_sem.at[c, src], row=sib)

    def x_arrival(c, src):
        block = xg.at[c, rows(src)]
        return remote(block, block, xf_sem.at[c, 0], xr_sem.at[c, src], row=sib)

    for c in range(n_chunk):
        for k in range(1, n_chip):
            x_send(c, k).start()
        x_sib(c).start()

    tiles[tile_slots] = jnp.zeros((tile, tile), bf16)
    tiles_copy.wait()

    def dense_row(i, carry):
        for j in range(col_tiles):
            value = tiles[slot_ref[i * col_tiles + j]]
            a_blk[pl.ds(pl.multiple_of(i * tile, tile), tile), pl.ds(j * tile, tile)] = value
        return carry

    lax.fori_loop(0, row_tiles, dense_row, 0)

    def p_send(c, k):
        dest = other_col(k)
        return remote(part.at[c, rows(dest)], part_in.at[c, me_c], ps_sem.at[c, k - 1],
                      pr_sem.at[c, me_c], col=dest)

    def p_arrival(c, src):
        block = part_in.at[c, src]
        return remote(block, block, ps_sem.at[c, 0], pr_sem.at[c, src], col=src)

    for c in range(n_chunk):
        x_local(c).wait()
        for k in range(1, n_chip):
            x_arrival(c, 2 * other_chip(n_chip - k) + core).wait_recv()
            x_forward(c, k).start()
        x_arrival(c, sib).wait_recv()
        for k in range(1, n_chip):
            x_arrival(c, 2 * other_chip(n_chip - k) + 1 - core).wait_recv()

        def forward_block(k, carry):
            dest = other_col(k)
            part[c, rows(dest), :] = jnp.dot(
                a_blk[rows(dest), :], xg[c], preferred_element_type=f32).astype(bf16)
            p_send(c, k).start()
            return carry

        lax.fori_loop(1, n_col, forward_block, 0)
        own[c] = jnp.dot(a_blk[rows(me_c), :], xg[c], preferred_element_type=f32)

    def dense_col(j, carry):
        for i in range(row_tiles):
            value = tiles[slot_ref[i * col_tiles + j]]
            at_blk[pl.ds(pl.multiple_of(j * tile, tile), tile), pl.ds(i * tile, tile)] = value.T
        return carry

    lax.fori_loop(0, col_tiles, dense_col, 0)

    w_copy.wait()
    ct_copy.wait()
    for c in range(n_chunk):
        total = own[c]
        for k in range(1, n_col):
            src = other_col(k)
            p_arrival(c, src).wait_recv()
            total = total + part_in[c, src].astype(f32)
        agg[:, pl.ds(c * width, width)] = total.astype(bf16)

    pre = jnp.dot(agg[...], w_ref[...], preferred_element_type=f32) + bias_ref[...]
    sig = jax.nn.sigmoid(pre)
    grad_pre = (ct_ref[...].astype(f32) * sig * (1.0 + pre * (1.0 - sig))).astype(bf16)
    gp_ref[...] = grad_pre
    out_ref[...] = (pre * sig).astype(bf16)

    def g_send(c, k):
        block = gg.at[c, rows(me_c)]
        return remote(block, block, gs_sem.at[c, k - 1], gr_sem.at[c, me_c], col=other_col(k))

    def g_arrival(c, src):
        block = gg.at[c, rows(src)]
        return remote(block, block, gs_sem.at[c, 0], gr_sem.at[c, src], col=src)

    for c in range(n_chunk):
        gg[c, rows(me_c), :] = lax.dot_general(
            gp_ref[...], w_ref[pl.ds(c * width, width), :], (((1,), (1,)), ((), ())),
            preferred_element_type=f32).astype(bf16)
        for k in range(1, n_col):
            g_send(c, k).start()

    bias_sum = jnp.sum(gp_ref[...].astype(f32), axis=0, keepdims=True)

    def bias_rows(value):
        high = value.astype(bf16).astype(f32)
        low = value - high
        index = lax.broadcasted_iota(jnp.int32, (BIAS_ROWS, features), 0)
        block = jnp.where(index == 0, high, jnp.where(index == 1, low, 0.0))
        return block.astype(bf16)

    bias_block = bias_rows(bias_sum)
    w_local = lax.dot_general(agg[...], gp_ref[...], (((0,), (0,)), ((), ())),
                              preferred_element_type=f32)
    for r in range(n_row):
        wb_out[r, pl.ds(0, w_rows)] = w_local[r * w_rows:(r + 1) * w_rows].astype(bf16)
        wb_out[r, pl.ds(w_rows, BIAS_ROWS)] = bias_block

    def w_send(k):
        dest = other_row(k)
        return remote(wb_out.at[dest], wb_in.at[me_r], ws_sem.at[k - 1], wr_sem.at[me_r], row=dest)

    def w_arrival(src):
        return remote(wb_in.at[src], wb_in.at[src], ws_sem.at[0], wr_sem.at[src], row=src)

    for k in range(1, n_row):
        w_send(k).start()
    wb_in[me_r] = wb_out[me_r]
    for k in range(1, n_row):
        w_arrival(other_row(k)).wait_recv()

    def add_up(ref, count):
        total = ref[0].astype(f32)
        for i in range(1, count):
            total = total + ref[i].astype(f32)
        return total[:w_rows], total[w_rows:w_rows + 1] + total[w_rows + 1:w_rows + 2]

    w_sum, b_sum = add_up(wb_in, n_row)
    wz[me_c, pl.ds(0, w_rows)] = w_sum.astype(bf16)
    wz[me_c, pl.ds(w_rows, BIAS_ROWS)] = bias_rows(b_sum)

    def z_send(k):
        return remote(wz.at[me_c], wz.at[me_c], zs_sem.at[k - 1], zr_sem.at[me_c], col=other_col(k))

    def z_arrival(src):
        return remote(wz.at[src], wz.at[src], zs_sem.at[0], zr_sem.at[src], col=src)

    for k in range(1, n_col):
        z_send(k).start()

    def s_send(c, i):
        return remote(xg.at[c, rows(i)], sib_in.at[c, i], ss_sem.at[c, i], sr_sem.at[c, i], row=sib)

    def t_send(c, k):
        dest = other_chip(k)
        return remote(xg.at[c, rows(n_chip + dest)], tot_in.at[c, chip], ts_sem.at[c, k - 1],
                      tr_sem.at[c, chip], row=2 * dest + core)

    def t_arrival(c, src):
        block = tot_in.at[c, src]
        return remote(block, block, ts_sem.at[c, 0], tr_sem.at[c, src], row=2 * src + core)

    def f_send(k):
        block = wfin.at[me_r]
        return remote(block, block, fs_sem.at[k - 1], fr_sem.at[me_r], row=other_row(k))

    def f_arrival(src):
        return remote(wfin.at[src], wfin.at[src], fs_sem.at[0], fr_sem.at[src], row=src)

    for c in range(n_chunk):
        for k in range(1, n_chip):
            x_forward(c, k).wait_send()

    for c in range(n_chunk):
        for k in range(1, n_col):
            g_arrival(c, other_col(k)).wait_recv()

        def sibling_block(k, carry):
            i = other_chip(k)
            xg[c, rows(i), :] = jnp.dot(at_blk[rows(2 * i + 1 - core), :], gg[c],
                                    preferred_element_type=f32).astype(bf16)
            s_send(c, i).start()
            return carry

        lax.fori_loop(1, n_chip + 1, sibling_block, 0)

        def chip_block(k, carry):
            i = other_chip(k)
            value = jnp.dot(at_blk[rows(2 * i + core), :], gg[c], preferred_element_type=f32)
            s_send(c, i).wait_recv()
            xg[c, rows(n_chip + i), :] = (value + sib_in[c, i].astype(f32)).astype(bf16)
            t_send(c, k).start()
            return carry

        lax.fori_loop(1, n_chip, chip_block, 0)
        value = jnp.dot(at_blk[rows(2 * chip + core), :], gg[c], preferred_element_type=f32)
        s_send(c, chip).wait_recv()
        own[c] = value + sib_in[c, chip].astype(f32)

        if c == 0:
            for k in range(1, n_col):
                z_arrival(other_col(k)).wait_recv()
            w_sum, b_sum = add_up(wz, n_col)
            wfin[me_r] = w_sum.astype(bf16)
            bg_ref[...] = b_sum
            for k in range(1, n_row):
                f_send(k).start()

    for c in range(n_chunk):
        total = own[c]
        for k in range(1, n_chip):
            src = other_chip(k)
            t_arrival(c, src).wait_recv()
            total = total + tot_in[c, src].astype(f32)
        fg_ref[:, pl.ds(c * width, width)] = total.astype(bf16)

    for k in range(1, n_row):
        f_arrival(other_row(k)).wait_recv()
    for r in range(n_row):
        wg_ref[pl.ds(r * w_rows, w_rows)] = wfin[r].astype(f32)

    for c in range(n_chunk):
        x_sib(c).wait_send()
        for k in range(1, n_chip):
            x_send(c, k).wait_send()
            t_send(c, k).wait_send()
        for k in range(1, n_col):
            p_send(c, k).wait_send()
            g_send(c, k).wait_send()
        for i in range(n_chip):
            s_send(c, i).wait_send()
    for k in range(1, n_row):
        w_send(k).wait_send()
        f_send(k).wait_send()
    for k in range(1, n_col):
        z_send(k).wait_send()


def per_device(n_row, n_col, node_features, tile_values, tile_rows, tile_cols, tile_count,
               weight, bias, cotangent):
    bf16, f32 = jnp.bfloat16, jnp.float32
    blocks = tile_values[0]
    slots, tile = blocks.shape[0], blocks.shape[-1]
    length, features = node_features.shape
    n_chunk = 2
    width = features // n_chunk
    n_chip = n_row // 2
    row_nodes, col_nodes = length * n_col, length * n_row
    row_tiles, col_tiles = row_nodes // tile, col_nodes // tile
    w_rows = features // n_row
    padded = w_rows + BIAS_ROWS

    slot_number = jnp.arange(slots, dtype=jnp.int32)
    place = jnp.where(slot_number < tile_count[0, 0],
                      tile_rows[0] * col_tiles + tile_cols[0], -1)
    hit = place[None, :] == jnp.arange(row_tiles * col_tiles, dtype=jnp.int32)[:, None]
    slot_map = jnp.min(jnp.where(hit, slot_number[None, :], slots), axis=1)

    dma = pltpu.SemaphoreType.DMA
    vmem = pl.BlockSpec(memory_space=pltpu.VMEM)
    anywhere = pl.BlockSpec(memory_space=pl.ANY)
    output, feature_grad, weight_sum, bias_sum = pl.pallas_call(
        functools.partial(layer_kernel, n_row, n_col, n_chunk),
        out_shape=(
            jax.ShapeDtypeStruct((length, features), bf16),
            jax.ShapeDtypeStruct((length, features), bf16),
            jax.ShapeDtypeStruct((features, features), f32),
            jax.ShapeDtypeStruct((1, features), f32),
        ),
        in_specs=[pl.BlockSpec(memory_space=pltpu.SMEM), anywhere, anywhere, anywhere, vmem, anywhere],
        out_specs=(vmem,) * 4,
        scratch_shapes=[
            pltpu.VMEM((slots + 1, tile, tile), bf16),
            pltpu.VMEM((row_nodes, col_nodes), bf16),
            pltpu.VMEM((col_nodes, row_nodes), bf16),
            pltpu.VMEM((features, features), bf16),
            pltpu.VMEM((length, features), bf16),
            pltpu.VMEM((n_chunk, col_nodes, width), bf16),
            pltpu.VMEM((n_chunk, row_nodes, width), bf16),
            pltpu.VMEM((n_chunk, n_col, length, width), bf16),
            pltpu.VMEM((n_chunk, length, width), f32),
            pltpu.VMEM((length, features), bf16),
            pltpu.VMEM((length, features), bf16),
            pltpu.VMEM((n_chunk, row_nodes, width), bf16),
            pltpu.VMEM((n_chunk, n_chip, length, width), bf16),
            pltpu.VMEM((n_chunk, n_chip, length, width), bf16),
            pltpu.VMEM((n_row, padded, features), bf16),
            pltpu.VMEM((n_row, padded, features), bf16),
            pltpu.VMEM((n_col, padded, features), bf16),
            pltpu.VMEM((n_row, w_rows, features), bf16),
            dma((3,)),
            dma((n_chunk,)),
            dma((n_chunk, n_chip)),
            dma((n_chunk, n_chip)),
            dma((n_chunk, n_row)),
            dma((n_chunk, n_col)),
            dma((n_chunk, n_col)),
            dma((n_chunk, n_col)),
            dma((n_chunk, n_col)),
            dma((n_chunk, n_chip)),
            dma((n_chunk, n_chip)),
            dma((n_chunk, n_chip)),
            dma((n_chunk, n_chip)),
            dma((n_row,)),
            dma((n_row,)),
            dma((n_col,)),
            dma((n_col,)),
            dma((n_row,)),
            dma((n_row,)),
        ],
        compiler_params=pltpu.CompilerParams(
            collective_id=0, has_side_effects=True, vmem_limit_bytes=62 * 1024 * 1024),
    )(slot_map, node_features, blocks, weight, bias[None, :], cotangent)
    grad_scale = 1.0 / math.sqrt(length * n_row * n_col)
    return output, feature_grad, weight_sum * grad_scale, bias_sum[0] * grad_scale


def solution(mesh):
    return jax.shard_map(
        functools.partial(per_device, mesh.shape["row"], mesh.shape["col"]),
        mesh=mesh,
        in_specs=(
            P(("col", "row"), None),
            P("row", "col", None, None),
            P("row", "col"),
            P("row", "col"),
            P("row", "col"),
            P(),
            P(),
            P(("row", "col"), None),
        ),
        out_specs=(P(("row", "col"), None), P(("col", "row"), None), P(), P()),
        check_vma=False,
    )
```

time: 349 us -> 93.8 us (0.27)
  waiting for transfers between devices: 184 us -> 0 us
  Pallas kernels: 0 us -> 85.1 us
  other arithmetic: 58 us -> 4.89 us
  blocking collectives: 39.5 us -> 0 us
  matrix products: 28.9 us -> 0 us
  local copies, waits for them, and re-layouts: 22.4 us -> 1.41 us
  between operations: 14.5 us -> 1.31 us
    reduce_scatter x2 -> x0, waiting for transfers between devices: 85.4 us -> none  [the longest x1 43.8 us: per_device(): lax.psum_scatter(partial_value, 'col', scatter_dimension=0, tiled=True)]
    pallas_call x0 -> x1, Pallas kernels: none -> 85.1 us  [per_device(): pl.pallas_call(functools.partial(layer_kernel, n_row, n_col, n_chunk), ou...]
    all_gather x2 -> x0, waiting for transfers between devices: 56.3 us -> none  [the longest x1 31.9 us: per_device(): node_panel = lax.all_gather(node_features, 'row', axis=0, tiled=True)]
    scatter-add x6 -> x0, other arithmetic: 46.8 us -> none  [step(): return running.at[target].add(product)]
    psum x1 -> x0, waiting for transfers between devices: 41.9 us -> none  [per_device(): weight_sum, bias_sum = lax.psum((weight_local, bias_local), ('row', 'col'))]
    psum x1 -> x0, blocking collectives: 39.5 us -> none  [per_device(): weight_sum, bias_sum = lax.psum((weight_local, bias_local), ('row', 'col'))]
    dot_general x9 -> x0, matrix products: 28.9 us -> none  [the longest x6 24.3 us: step(): jnp.einsum(einsum_form, tile_piece, panels[source], preferred_element_typ...]
    gather x6 -> x0, local copies, waits for them, and re-layouts: 16.6 us -> none  [step(): panels[source]]
  transfers between devices with their start and end apart: 5 -> 0, of which waited for: 5 -> 0; matrix products, arithmetic and copies ran while one was open for 17% -> 0% of each run, Pallas kernels for 0% -> 0%
where the time goes in v1:
time: 93.8 us; the launch traced here: 92.7 us
  Pallas kernels  85.1 us (91%)
  other arithmetic  4.89 us (5%)
  local copies, waits for them, and re-layouts  1.41 us (2%)
  between operations  1.31 us (1%)
    pallas_call x1, Pallas kernels, per_device(): pl.pallas_call(functools.partial(layer_kernel, n_row, n_col, n_chunk), ou...  85.1 us
    mul x1, other arithmetic, per_device(): weight_sum * grad_scale  2.3 us

profile of v1, /device:TPU:0, one launch (start us, length us, event | category | flops | bytes accessed | tf_op | source)
XLA Modules:
  0.0 92.7 jit_solution(10588282067284990924)
XLA Ops:
  1.3 0.7 fusion
  2.0 0.6 select_reduce_fusion.slot_ref
  2.6 85.1 %shard_map.111 = (bf16[256,512]{1,0:T(8,128)(2,1)}, bf16[256,512]{1,0:T(8,128)(2,1)}, f32[512,512]{1,0:T(8,128)}, f32[1,512]{1,0:T(1,128)}) custom-call(s32[128]{0:T(128)} %select_reduce_fusion.slot_ref, bf16[256,512]{1,0:T(8,128)(2,1)} %x_ref.1, bf16[48,128,128]{2,1,0:T(8,128)(2,1)} %bitcast.7, bf16[512,512]{1,0:T(8,128)(2,1)} %w_hbm.1, f32[1,512]{1,0:T(1,128)} %bitcast.8, ...), custom_call_target="tpu_custom_call" | custom-call | tf_op jit(solution)/shard_map/pallas_call | solution.py:337
  87.7 0.0 copy-start.1
  87.7 0.0 copy-start
  87.7 1.3 %broadcast_multiply_fusion.1 = f32[1,512]{1,0:T(1,128)} fusion(f32[1,512]{1,0:T(1,128)} %get-tuple-element.11), kind=kLoop, calls=%fused_computation.4 | loop fusion | flops 512 | bytes 4096 | tf_op jit(solution)/shard_map/mul | solution.py:390
  89.0 2.3 %broadcast_multiply_fusion = f32[512,512]{1,0:T(8,128)} fusion(f32[512,512]{1,0:T(8,128)} %get-tuple-element.10), kind=kLoop, calls=%fused_computation | loop fusion | flops 262144 | bytes 2097152 | tf_op jit(solution)/shard_map/mul | solution.py:390
  91.3 0.0 copy-done.1
  91.3 0.7 copy.15
  92.0 0.0 copy-done
  92.0 0.7 copy.16
Async XLA Ops:
  87.7 3.6 %copy-start.1 = (bf16[256,512]{1,0:T(8,128)(2,1)S(1)}, bf16[256,512]{1,0:T(8,128)(2,1)}, u32[]{:S(2)}) copy-start(bf16[256,512]{1,0:T(8,128)(2,1)} %get-tuple-element.16) | copy-start | bytes 786436
  87.7 4.3 %copy-start = (bf16[256,512]{1,0:T(8,128)(2,1)S(1)}, bf16[256,512]{1,0:T(8,128)(2,1)}, u32[]{:S(2)}) copy-start(bf16[256,512]{1,0:T(8,128)(2,1)} %get-tuple-element.17) | copy-start | bytes 786436

commit v2 on v1

--- a/solution.py
+++ b/solution.py
@@ -16,7 +16,7 @@
     n_row, n_col, n_chunk,
     slot_ref, x_ref, tiles_hbm, w_hbm, bias_ref, ct_hbm,
     out_ref, fg_ref, wg_ref, bg_ref,
-    tiles, a_blk, at_blk, w_ref, ct_ref, xg, part, part_in, own, agg, gp_ref, gg,
+    tiles, a_blk, at_blk, w_ref, ct_ref, xg, part, part_in, own, agg_sum, agg, gp_ref, gg,
     sib_in, tot_in, wb_out, wb_in, wz, wfin,
     local_sem, xl_sem, xs_sem, xf_sem, xr_sem, ps_sem, pr_sem, gs_sem, gr_sem,
     ss_sem, sr_sem, ts_sem, tr_sem, ws_sem, wr_sem, zs_sem, zr_sem, fs_sem, fr_sem,
@@ -30,6 +30,7 @@
     col_tiles = length * n_row // tile
     n_chip = n_row // 2
     w_rows = features // n_row
+    scale = 1.0 / math.sqrt(length * n_row * n_col)
 
     me_r, me_c = lax.axis_index("row"), lax.axis_index("col")
     chip, core = me_r // 2, me_r % 2
@@ -108,14 +109,36 @@
 
     lax.fori_loop(0, row_tiles, dense_row, 0)
 
-    def p_send(c, k):
-        dest = other_col(k)
-        return remote(part.at[c, rows(dest)], part_in.at[c, me_c], ps_sem.at[c, k - 1],
-                      pr_sem.at[c, me_c], col=dest)
-
-    def p_arrival(c, src):
-        block = part_in.at[c, src]
-        return remote(block, block, ps_sem.at[c, 0], pr_sem.at[c, src], col=src)
+    flip = (me_c >= n_col // 2).astype(jnp.int32)
+
+    def mirrored(i):
+        return i + flip * (n_col - 1 - 2 * i)
+
+    place = mirrored(me_c)
+
+    def p_send(c, dest):
+        up = (dest > me_c).astype(jnp.int32)
+        slot = jnp.where(dest == me_c - 1, n_col, dest)
+        return remote(part.at[c, rows(dest)], part_in.at[c, slot], ps_sem.at[c, dest],
+                      pr_sem.at[c, slot], col=me_c + 2 * up - 1)
+
+    def p_arrival(c, slot):
+        block = part_in.at[c, slot]
+        return remote(block, block, ps_sem.at[c, 0], pr_sem.at[c, slot], col=other_col(1))
+
+    def pass_on(c, dest, first):
+        value = jnp.dot(a_blk[rows(dest), :], xg[c], preferred_element_type=f32)
+
+        @pl.when(first)
+        def _():
+            part[c, rows(dest), :] = value.astype(bf16)
+
+        @pl.when(jnp.logical_not(first))
+        def _():
+            p_arrival(c, dest).wait_recv()
+            part[c, rows(dest), :] = (value + part_in[c, dest].astype(f32)).astype(bf16)
+
+        p_send(c, dest).start()
 
     for c in range(n_chunk):
         x_local(c).wait()
@@ -127,10 +150,14 @@
             x_arrival(c, 2 * other_chip(n_chip - k) + 1 - core).wait_recv()
 
         def forward_block(k, carry):
-            dest = other_col(k)
-            part[c, rows(dest), :] = jnp.dot(
-                a_blk[rows(dest), :], xg[c], preferred_element_type=f32).astype(bf16)
-            p_send(c, k).start()
+            @pl.when(n_col - k > place)
+            def _():
+                pass_on(c, mirrored(n_col - k), place == 0)
+
+            @pl.when(k - 1 < place)
+            def _():
+                pass_on(c, mirrored(k - 1), place == n_col - 1)
+
             return carry
 
         lax.fori_loop(1, n_col, forward_block, 0)
@@ -147,11 +174,19 @@
     w_copy.wait()
     ct_copy.wait()
     for c in range(n_chunk):
-        total = own[c]
-        for k in range(1, n_col):
-            src = other_col(k)
-            p_arrival(c, src).wait_recv()
-            total = total + part_in[c, src].astype(f32)
+        agg_sum[...] = own[c]
+
+        @pl.when(me_c > 0)
+        def _():
+            p_arrival(c, me_c).wait_recv()
+            agg_sum[...] += part_in[c, me_c].astype(f32)
+
+        @pl.when(me_c < n_col - 1)
+        def _():
+            p_arrival(c, n_col).wait_recv()
+            agg_sum[...] += part_in[c, n_col].astype(f32)
+
+        total = agg_sum[...]
         agg[:, pl.ds(c * width, width)] = total.astype(bf16)
 
     pre = jnp.dot(agg[...], w_ref[...], preferred_element_type=f32) + bias_ref[...]
@@ -160,20 +195,57 @@
     gp_ref[...] = grad_pre
     out_ref[...] = (pre * sig).astype(bf16)
 
-    def g_send(c, k):
-        block = gg.at[c, rows(me_c)]
-        return remote(block, block, gs_sem.at[c, k - 1], gr_sem.at[c, me_c], col=other_col(k))
+    def g_send(c, src, step):
+        block = gg.at[c, rows(src)]
+        slot = jnp.where((src == me_c) & (step < 0), n_col, src)
+        return remote(block, block, gs_sem.at[c, slot], gr_sem.at[c, src], col=me_c + step)
 
     def g_arrival(c, src):
         block = gg.at[c, rows(src)]
-        return remote(block, block, gs_sem.at[c, 0], gr_sem.at[c, src], col=src)
+        return remote(block, block, gs_sem.at[c, 0], gr_sem.at[c, src], col=other_col(1))
+
+    has_right, has_left = me_c < n_col - 1, me_c > 0
+
+    def g_own(c, act):
+        @pl.when(has_right)
+        def _():
+            act(g_send(c, me_c, 1))
+
+        @pl.when(has_left)
+        def _():
+            act(g_send(c, me_c, -1))
+
+    def start(copy):
+        copy.start()
+
+    def sent(copy):
+        copy.wait_send()
+
+    def g_from(c, k, arrive, act):
+        @pl.when(me_c - k >= 0)
+        def _():
+            if arrive:
+                g_arrival(c, me_c - k).wait_recv()
+
+            @pl.when(has_right)
+            def _():
+                act(g_send(c, me_c - k, 1))
+
+        @pl.when(me_c + k < n_col)
+        def _():
+            if arrive:
+                g_arrival(c, me_c + k).wait_recv()
+
+            @pl.when(has_left)
+            def _():
+                act(g_send(c, me_c + k, -1))
 
     for c in range(n_chunk):
         gg[c, rows(me_c), :] = lax.dot_general(
             gp_ref[...], w_ref[pl.ds(c * width, width), :], (((1,), (1,)), ((), ())),
             preferred_element_type=f32).astype(bf16)
-        for k in range(1, n_col):
-            g_send(c, k).start()
+        if c == 0:
+            g_own(c, start)
 
     bias_sum = jnp.sum(gp_ref[...].astype(f32), axis=0, keepdims=True)
 
@@ -201,27 +273,59 @@
     for k in range(1, n_row):
         w_send(k).start()
     wb_in[me_r] = wb_out[me_r]
-    for k in range(1, n_row):
-        w_arrival(other_row(k)).wait_recv()
-
     def add_up(ref, count):
         total = ref[0].astype(f32)
         for i in range(1, count):
             total = total + ref[i].astype(f32)
         return total[:w_rows], total[w_rows:w_rows + 1] + total[w_rows + 1:w_rows + 2]
 
-    w_sum, b_sum = add_up(wb_in, n_row)
-    wz[me_c, pl.ds(0, w_rows)] = w_sum.astype(bf16)
-    wz[me_c, pl.ds(w_rows, BIAS_ROWS)] = bias_rows(b_sum)
-
-    def z_send(k):
-        return remote(wz.at[me_c], wz.at[me_c], zs_sem.at[k - 1], zr_sem.at[me_c], col=other_col(k))
+    root = n_col // 2
+
+    def store_term(ref, index, value):
+        w_part, b_part = value
+        ref[index, pl.ds(0, w_rows)] = w_part.astype(bf16)
+        ref[index, pl.ds(w_rows, BIAS_ROWS)] = bias_rows(b_part)
+
+    def z_send():
+        return remote(wz.at[me_c], wz.at[me_c], zs_sem.at[n_col], zr_sem.at[me_c], col=root)
 
     def z_arrival(src):
         return remote(wz.at[src], wz.at[src], zs_sem.at[0], zr_sem.at[src], col=src)
 
-    for k in range(1, n_col):
-        z_send(k).start()
+    def z_back(dest):
+        return remote(wz.at[n_col], wz.at[n_col], zs_sem.at[dest], zr_sem.at[n_col], col=dest)
+
+    def others_of_root(act):
+        for i in range(n_col):
+            if i != root:
+                act(i)
+
+    def reduce_rows():
+        for k in range(1, n_row):
+            w_arrival(other_row(k)).wait_recv()
+        store_term(wz, me_c, add_up(wb_in, n_row))
+
+        @pl.when(me_c != root)
+        def _():
+            z_send().start()
+
+    def reduce_cols():
+        @pl.when(me_c == root)
+        def _():
+            others_of_root(lambda i: z_arrival(i).wait_recv())
+            store_term(wz, n_col, add_up(wz, n_col))
+            others_of_root(lambda i: z_back(i).start())
+
+    def gather_rows():
+        @pl.when(me_c != root)
+        def _():
+            z_back(other_col(1)).wait_recv()
+
+        wfin[me_r] = wz[n_col, pl.ds(0, w_rows)]
+        last = wz[n_col, pl.ds(w_rows, BIAS_ROWS)].astype(f32)
+        bg_ref[...] = (last[0:1] + last[1:2]) * scale
+        for k in range(1, n_row):
+            f_send(k).start()
 
     def s_send(c, i):
         return remote(xg.at[c, rows(i)], sib_in.at[c, i], ss_sem.at[c, i], sr_sem.at[c, i], row=sib)
@@ -246,20 +350,18 @@
         for k in range(1, n_chip):
             x_forward(c, k).wait_send()
 
-    for c in range(n_chunk):
-        for k in range(1, n_col):
-            g_arrival(c, other_col(k)).wait_recv()
-
-        def sibling_block(k, carry):
+    def sibling_blocks(c):
+        def one(k, carry):
             i = other_chip(k)
             xg[c, rows(i), :] = jnp.dot(at_blk[rows(2 * i + 1 - core), :], gg[c],
-                                    preferred_element_type=f32).astype(bf16)
+                                        preferred_element_type=f32).astype(bf16)
             s_send(c, i).start()
             return carry
 
-        lax.fori_loop(1, n_chip + 1, sibling_block, 0)
-
-        def chip_block(k, carry):
+        lax.fori_loop(1, n_chip + 1, one, 0)
+
+    def chip_blocks(c):
+        def one(k, carry):
             i = other_chip(k)
             value = jnp.dot(at_blk[rows(2 * i + core), :], gg[c], preferred_element_type=f32)
             s_send(c, i).wait_recv()
@@ -267,19 +369,28 @@
             t_send(c, k).start()
             return carry
 
-        lax.fori_loop(1, n_chip, chip_block, 0)
+        lax.fori_loop(1, n_chip, one, 0)
         value = jnp.dot(at_blk[rows(2 * chip + core), :], gg[c], preferred_element_type=f32)
         s_send(c, chip).wait_recv()
         own[c] = value + sib_in[c, chip].astype(f32)
 
+    for c in range(n_chunk):
+        for k in range(1 if c == 0 else 2, n_col):
+            g_from(c, k, True, start)
+            if k == 1 and n_chunk > 1:
+                g_own(1, start)
         if c == 0:
-            for k in range(1, n_col):
-                z_arrival(other_col(k)).wait_recv()
-            w_sum, b_sum = add_up(wz, n_col)
-            wfin[me_r] = w_sum.astype(bf16)
-            bg_ref[...] = b_sum
-            for k in range(1, n_row):
-                f_send(k).start()
+            reduce_rows()
+        if c == n_chunk - 1:
+            gather_rows()
+        sibling_blocks(c)
+        if c + 1 < n_chunk:
+            g_from(c + 1, 1, True, start)
+            if c + 2 < n_chunk:
+                g_own(c + 2, start)
+        chip_blocks(c)
+        if c == 0:
+            reduce_cols()
 
     for c in range(n_chunk):
         total = own[c]
@@ -292,7 +403,7 @@
     for k in range(1, n_row):
         f_arrival(other_row(k)).wait_recv()
     for r in range(n_row):
-        wg_ref[pl.ds(r * w_rows, w_rows)] = wfin[r].astype(f32)
+        wg_ref[pl.ds(r * w_rows, w_rows)] = wfin[r].astype(f32) * scale
 
     for c in range(n_chunk):
         x_sib(c).wait_send()
@@ -300,15 +411,22 @@
             x_send(c, k).wait_send()
             t_send(c, k).wait_send()
         for k in range(1, n_col):
-            p_send(c, k).wait_send()
-            g_send(c, k).wait_send()
+            p_send(c, other_col(k)).wait_send()
+            g_from(c, k, False, sent)
+        g_own(c, sent)
         for i in range(n_chip):
             s_send(c, i).wait_send()
     for k in range(1, n_row):
         w_send(k).wait_send()
         f_send(k).wait_send()
-    for k in range(1, n_col):
-        z_send(k).wait_send()
+
+    @pl.when(me_c != root)
+    def _():
+        z_send().wait_send()
+
+    @pl.when(me_c == root)
+    def _():
+        others_of_root(lambda i: z_back(i).wait_send())
 
 
 def per_device(n_row, n_col, node_features, tile_values, tile_rows, tile_cols, tile_count,
@@ -334,7 +452,7 @@
     dma = pltpu.SemaphoreType.DMA
     vmem = pl.BlockSpec(memory_space=pltpu.VMEM)
     anywhere = pl.BlockSpec(memory_space=pl.ANY)
-    output, feature_grad, weight_sum, bias_sum = pl.pallas_call(
+    output, feature_grad, weight_grad, bias_grad = pl.pallas_call(
         functools.partial(layer_kernel, n_row, n_col, n_chunk),
         out_shape=(
             jax.ShapeDtypeStruct((length, features), bf16),
@@ -352,8 +470,9 @@
             pltpu.VMEM((length, features), bf16),
             pltpu.VMEM((n_chunk, col_nodes, width), bf16),
             pltpu.VMEM((n_chunk, row_nodes, width), bf16),
-            pltpu.VMEM((n_chunk, n_col, length, width), bf16),
+            pltpu.VMEM((n_chunk, n_col + 1, length, width), bf16),
             pltpu.VMEM((n_chunk, length, width), f32),
+            pltpu.VMEM((length, width), f32),
             pltpu.VMEM((length, features), bf16),
             pltpu.VMEM((length, features), bf16),
             pltpu.VMEM((n_chunk, row_nodes, width), bf16),
@@ -361,33 +480,32 @@
             pltpu.VMEM((n_chunk, n_chip, length, width), bf16),
             pltpu.VMEM((n_row, padded, features), bf16),
             pltpu.VMEM((n_row, padded, features), bf16),
-            pltpu.VMEM((n_col, padded, features), bf16),
+            pltpu.VMEM((n_col + 1, padded, features), bf16),
             pltpu.VMEM((n_row, w_rows, features), bf16),
             dma((3,)),
             dma((n_chunk,)),
             dma((n_chunk, n_chip)),
             dma((n_chunk, n_chip)),
             dma((n_chunk, n_row)),
-            dma((n_chunk, n_col)),
-            dma((n_chunk, n_col)),
-            dma((n_chunk, n_col)),
-            dma((n_chunk, n_col)),
+            dma((n_chunk, n_col + 1)),
+            dma((n_chunk, n_col + 1)),
+            dma((n_chunk, n_col + 1)),
+            dma((n_chunk, n_col + 1)),
             dma((n_chunk, n_chip)),
             dma((n_chunk, n_chip)),
             dma((n_chunk, n_chip)),
             dma((n_chunk, n_chip)),
             dma((n_row,)),
             dma((n_row,)),
-            dma((n_col,)),
-            dma((n_col,)),
+            dma((n_col + 1,)),
+            dma((n_col + 1,)),
             dma((n_row,)),
             dma((n_row,)),
         ],
         compiler_params=pltpu.CompilerParams(
             collective_id=0, has_side_effects=True, vmem_limit_bytes=62 * 1024 * 1024),
     )(slot_map, node_features, blocks, weight, bias[None, :], cotangent)
-    grad_scale = 1.0 / math.sqrt(length * n_row * n_col)
-    return output, feature_grad, weight_sum * grad_scale, bias_sum[0] * grad_scale
+    return output, feature_grad, weight_grad, bias_grad[0]
 
 
 def solution(mesh):

time: 93.8 us -> 86.9 us (0.926)
  Pallas kernels: 85.1 us -> 79.1 us
  other arithmetic: 4.89 us -> 1.28 us
  local copies, waits for them, and re-layouts: 1.41 us -> 4.98 us
    pallas_call x1, Pallas kernels: 85.1 us -> 79.1 us  [per_device(): pl.pallas_call(functools.partial(layer_kernel, n_row, n_col, n_chunk), ou...]
    mul x2 -> x0, other arithmetic: 3.61 us -> none  [the longest x1 2.3 us: per_device(): weight_sum * grad_scale]
    unnamed x6 -> x8, local copies, waits for them, and re-layouts: 1.41 us -> 4.98 us
where the time goes in v2:
time: 86.9 us; the launch traced here: 86.7 us
  Pallas kernels  79.1 us (91%)
  local copies, waits for them, and re-layouts  4.98 us (6%)
  between operations  1.31 us (2%)
  other arithmetic  1.28 us (1%)
    pallas_call x1, Pallas kernels, per_device(): pl.pallas_call(functools.partial(layer_kernel, n_row, n_col, n_chunk), ou...  79.1 us
    unnamed x8, local copies, waits for them, and re-layouts  4.98 us

profile of v2, /device:TPU:0, one launch (start us, length us, event | category | flops | bytes accessed | tf_op | source)
XLA Modules:
  0.0 86.7 jit_solution(10199766535916853741)
XLA Ops:
  1.3 0.7 fusion
  2.0 0.6 select_reduce_fusion.slot_ref
  2.6 79.1 %shard_map.111 = (bf16[256,512]{1,0:T(8,128)(2,1)}, bf16[256,512]{1,0:T(8,128)(2,1)}, f32[512,512]{1,0:T(8,128)}, f32[1,512]{1,0:T(1,128)}) custom-call(s32[128]{0:T(128)} %select_reduce_fusion.slot_ref, bf16[256,512]{1,0:T(8,128)(2,1)} %x_ref.1, bf16[48,128,128]{2,1,0:T(8,128)(2,1)} %bitcast.7, bf16[512,512]{1,0:T(8,128)(2,1)} %w_hbm.1, f32[1,512]{1,0:T(1,128)} %bitcast.8, ...), custom_call_target="tpu_custom_call" | custom-call | tf_op jit(solution)/shard_map/pallas_call | solution.py:455
  81.7 0.0 copy-start
  81.7 0.0 copy-start.1
  81.7 1.8 %copy.17 = bf16[256,512]{1,0:T(8,128)(2,1)} copy(bf16[256,512]{1,0:T(8,128)(2,1)} %get-tuple-element.16) | data formatting | bytes 524288
  83.4 1.7 %copy.18 = bf16[256,512]{1,0:T(8,128)(2,1)} copy(bf16[256,512]{1,0:T(8,128)(2,1)} %get-tuple-element.17) | data formatting | bytes 524288
  85.1 0.0 copy-done
  85.1 1.0 %copy.19 = f32[512,512]{1,0:T(8,128)} copy(f32[512,512]{1,0:T(8,128)S(1)} %copy-done) | data formatting | bytes 2097152
  86.1 0.0 copy-done.1
  86.1 0.6 copy.20
Async XLA Ops:
  81.7 3.4 %copy-start = (f32[512,512]{1,0:T(8,128)S(1)}, f32[512,512]{1,0:T(8,128)}, u32[]{:S(2)}) copy-start(f32[512,512]{1,0:T(8,128)} %get-tuple-element.18) | copy-start | bytes 3145732
  81.7 4.4 %copy-start.1 = (f32[1,512]{1,0:T(1,128)S(1)}, f32[1,512]{1,0:T(1,128)}, u32[]{:S(2)}) copy-start(f32[1,512]{1,0:T(1,128)} %get-tuple-element.11) | copy-start | bytes 6148

commit v3 on v2

--- a/solution.py
+++ b/solution.py
@@ -379,7 +379,7 @@
             g_from(c, k, True, start)
             if k == 1 and n_chunk > 1:
                 g_own(1, start)
-        if c == 0:
+        if c == 1:
             reduce_rows()
         if c == n_chunk - 1:
             gather_rows()
@@ -388,9 +388,9 @@
             g_from(c + 1, 1, True, start)
             if c + 2 < n_chunk:
                 g_own(c + 2, start)
+        if c == n_chunk - 2:
+            reduce_cols()
         chip_blocks(c)
-        if c == 0:
-            reduce_cols()
 
     for c in range(n_chunk):
         total = own[c]
@@ -429,13 +429,23 @@
         others_of_root(lambda i: z_back(i).wait_send())
 
 
+def copy_kernel(*refs):
+    sems = refs[-1]
+    count = (len(refs) - 1) // 2
+    copies = [pltpu.make_async_copy(refs[i], refs[count + i], sems.at[i]) for i in range(count)]
+    for copy in copies:
+        copy.start()
+    for copy in copies:
+        copy.wait()
+
+
 def per_device(n_row, n_col, node_features, tile_values, tile_rows, tile_cols, tile_count,
                weight, bias, cotangent):
     bf16, f32 = jnp.bfloat16, jnp.float32
     blocks = tile_values[0]
     slots, tile = blocks.shape[0], blocks.shape[-1]
     length, features = node_features.shape
-    n_chunk = 2
+    n_chunk = 4
     width = features // n_chunk
     n_chip = n_row // 2
     row_nodes, col_nodes = length * n_col, length * n_row
@@ -505,6 +515,15 @@
         compiler_params=pltpu.CompilerParams(
             collective_id=0, has_side_effects=True, vmem_limit_bytes=62 * 1024 * 1024),
     )(slot_map, node_features, blocks, weight, bias[None, :], cotangent)
+    results = (output, feature_grad, weight_grad, bias_grad)
+    output, feature_grad, weight_grad, bias_grad = pl.pallas_call(
+        copy_kernel,
+        out_shape=tuple(jax.ShapeDtypeStruct(r.shape, r.dtype) for r in results),
+        in_specs=[anywhere] * len(results),
+        out_specs=(anywhere,) * len(results),
+        scratch_shapes=[dma((len(results),))],
+        compiler_params=pltpu.CompilerParams(vmem_limit_bytes=62 * 1024 * 1024),
+    )(*results)
     return output, feature_grad, weight_grad, bias_grad[0]
 
 

time: 86.9 us -> 134 us (1.54)
  Pallas kernels: 79.1 us -> 131 us
  local copies, waits for them, and re-layouts: 4.98 us -> 0 us
    pallas_call x0 -> x1, Pallas kernels: none -> 48.8 us  [per_device(): pl.pallas_call(copy_kernel, out_shape=tuple((jax.ShapeDtypeStruct(r.shape...]
    unnamed x8 -> x0, local copies, waits for them, and re-layouts: 4.98 us -> none
    pallas_call x1, Pallas kernels: 79.1 us -> 82 us  [per_device(): pl.pallas_call(functools.partial(layer_kernel, n_row, n_col, n_chunk), ou...]
where the time goes in v3:
time: 134 us; the launch traced here: 133 us
  Pallas kernels  131 us (98%)
    pallas_call x1, Pallas kernels, per_device(): pl.pallas_call(functools.partial(layer_kernel, n_row, n_col, n_chunk), ou...  82 us
    pallas_call x1, Pallas kernels, per_device(): pl.pallas_call(copy_kernel, out_shape=tuple((jax.ShapeDtypeStruct(r.shape...  48.8 us

profile of v3, /device:TPU:0, one launch (start us, length us, event | category | flops | bytes accessed | tf_op | source)
XLA Modules:
  0.0 133.4 jit_solution(10028368386107613318)
XLA Ops:
  1.3 0.7 fusion
  2.0 0.6 select_reduce_fusion.slot_ref
  2.6 82.0 %shard_map.111 = (bf16[256,512]{1,0:T(8,128)(2,1)}, bf16[256,512]{1,0:T(8,128)(2,1)}, f32[512,512]{1,0:T(8,128)}, f32[1,512]{1,0:T(1,128)}) custom-call(s32[128]{0:T(128)} %select_reduce_fusion.slot_ref, bf16[256,512]{1,0:T(8,128)(2,1)} %x_ref.1, bf16[48,128,128]{2,1,0:T(8,128)(2,1)} %bitcast.7, bf16[512,512]{1,0:T(8,128)(2,1)} %w_hbm.1, f32[1,512]{1,0:T(1,128)} %bitcast.8, ...), custom_call_target="tpu_custom_call" | custom-call | tf_op jit(solution)/shard_map/pallas_call | solution.py:465
  84.5 48.8 %shard_map.112 = (bf16[256,512]{1,0:T(8,128)(2,1)}, bf16[256,512]{1,0:T(8,128)(2,1)}, f32[512,512]{1,0:T(8,128)}, f32[1,512]{1,0:T(1,128)}) custom-call(bf16[256,512]{1,0:T(8,128)(2,1)} %get-tuple-element.12.refs_0_, bf16[256,512]{1,0:T(8,128)(2,1)} %get-tuple-element.13.refs_1_, f32[512,512]{1,0:T(8,128)} %get-tuple-element.14.refs_2_, ...), custom_call_target="tpu_custom_call" | custom-call | tf_op jit(solution)/shard_map/pallas_call | solution.py:519
